TPU v7x, 32 devices: a whole 2x2x4 slice. The times are simulated.
32 devices in a mesh: front: 4 (over z), row: 4 (over y, core), col: 2 (over x).
Axes of the slice: x: 2, y: 2, z: 4, core: 2. Of those that a mesh axis runs over, the one named last changes fastest.
Arguments:
- pivot_block: float32 [8, 512, 512], P(('front', 'col'), 'row'), as said below
- panel_rows: float32 [8, 4096, 512], P(('front', 'col'), 'row'), may hold values from -0.875 to 0.875
- update_block: float32 [8, 4096, 4096], P(('front', 'col'), 'row'), as said below
- tile_map: int32 [8, 32], replicated, may hold values from 0 to 95, as said below
Outputs:
- pivot_factor: float32 [8, 512, 512], P(('front', 'col'), 'row')
- panel_factor: float32 [8, 4096, 512], P(('front', 'col'), 'row')
- parent_update: float32 [2, 12288, 12288], P('col', 'front', 'row')
Inputs may be any that keep to these rules, and one draw needn't show every extreme that they name: `pivot_block`: each child's pivot block is symmetric positive definite. `update_block`: each child's update block is symmetric. `tile_map`: row c lists, strictly increasing, the parent tiles that receive child c's 32 tiles; child c belongs to parent c % 2. At most 9 entries of one row fall in any aligned block of 24 parent tiles, and exactly 9 do in some block.
All inputs are finite; a program needn't handle non-finite values.
Results may differ from a plain program's by a relative error of at most 0.0001.
Values sent between devices are 32-bit elements; how exact they have to be, the bound alone decides.
A program may use at most 192 MiB of HBM per device.

v0:
```python
import jax
import jax.numpy as jnp
from jax import lax
from jax.sharding import PartitionSpec as P

TILE = 128
PARENT = 12288


def solve_panel(lower_factor, panel_block):
    return jax.scipy.linalg.solve_triangular(lower_factor, panel_block.T, lower=True).T


def block_slots(tile_ids, block_count, block_width, slot_count):
    owners = tile_ids // block_width
    block_ids = jnp.arange(block_count, dtype=jnp.int32)
    starts = jnp.sum((owners[None, :] < block_ids[:, None]).astype(jnp.int32), axis=1)
    counts = jnp.sum((owners[None, :] == block_ids[:, None]).astype(jnp.int32), axis=1)
    slot_ids = jnp.arange(slot_count, dtype=jnp.int32)
    picks = jnp.minimum(starts[:, None] + slot_ids[None, :], tile_ids.shape[0] - 1)
    usable = slot_ids[None, :] < counts[:, None]
    return (picks, usable)


def local_onehot(child_maps, block_me, block_width, slot_count):
    owners = child_maps // block_width
    starts = jnp.sum((owners < block_me).astype(jnp.int32), axis=1)
    counts = jnp.sum((owners == block_me).astype(jnp.int32), axis=1)
    slot_ids = jnp.arange(slot_count, dtype=jnp.int32)
    picks = jnp.minimum(starts[:, None] + slot_ids[None, :], child_maps.shape[1] - 1)
    local_tile = jnp.take_along_axis(child_maps, picks, axis=1) - block_me * block_width
    usable = slot_ids[None, :] < counts[:, None]
    targets = jnp.arange(block_width, dtype=jnp.int32)
    onehot = (local_tile[:, None, :] == targets[None, :, None]) & usable[:, None, :]
    return onehot.astype(jnp.float32)


def local(pivot_block, panel_rows, update_block, tile_map):
    row_count = lax.axis_size("row")
    front_count = lax.axis_size("front")
    col_count = lax.axis_size("col")
    row_me = lax.axis_index("row")
    front_me = lax.axis_index("front")
    col_me = lax.axis_index("col")
    tile_size = TILE
    pivot_share = pivot_block.shape[1]
    own_rows = panel_rows.shape[1]
    contrib_order = update_block.shape[2]
    tile_count = contrib_order // tile_size
    block_width = PARENT // tile_size // row_count
    slot_count = tile_count // row_count + 1
    child_index = front_me * col_count + col_me
    tile_ids = lax.dynamic_index_in_dim(tile_map, child_index, 0, keepdims=False)
    pivot_whole = lax.all_gather(pivot_block[0], "row", axis=0, tiled=True)
    lower_factor = jnp.linalg.cholesky(pivot_whole)
    own_factor = solve_panel(lower_factor, panel_rows[0])
    all_factor = lax.all_gather(own_factor, "row", axis=0, tiled=True)
    col_picks, col_usable = block_slots(tile_ids, row_count, block_width, slot_count)
    contribution = update_block[0] - jnp.dot(
        own_factor, all_factor.T, precision=lax.Precision.HIGHEST
    )
    shaped = contribution.reshape(own_rows, tile_count, tile_size)
    picked = jnp.take(shaped, col_picks.reshape(-1), axis=1)
    picked = picked.reshape(own_rows, row_count, slot_count, tile_size)
    source = jnp.where(col_usable[None, :, :, None], picked, 0.0)
    arrived = lax.all_to_all(source, "row", split_axis=1, concat_axis=0, tiled=True)
    arrived = arrived.reshape(contrib_order, slot_count, tile_size)
    row_picks, row_usable = block_slots(tile_ids, front_count, block_width, slot_count)
    shaped = arrived.reshape(tile_count, tile_size, slot_count, tile_size)
    picked = jnp.take(shaped, row_picks.reshape(-1), axis=0)
    picked = picked.reshape(front_count, slot_count, tile_size, slot_count, tile_size)
    picked = jnp.where(row_usable[:, :, None, None, None], picked, 0.0)
    routed = lax.all_to_all(picked, "front", split_axis=0, concat_axis=0, tiled=True)
    sources = jnp.arange(front_count, dtype=jnp.int32) * col_count + col_me
    child_maps = jnp.take(tile_map, sources, axis=0)
    row_hot = local_onehot(child_maps, front_me, block_width, slot_count)
    col_hot = local_onehot(child_maps, row_me, block_width, slot_count)
    partial_value = jnp.einsum("fsxty,fbt->fsxby", routed, col_hot, precision=lax.Precision.HIGHEST)
    parent = jnp.einsum("fas,fsxby->axby", row_hot, partial_value, precision=lax.Precision.HIGHEST)
    parent = parent.reshape(block_width * tile_size, block_width * tile_size)
    pivot_rows_out = lax.dynamic_slice_in_dim(lower_factor, row_me * pivot_share, pivot_share, 0)
    return (pivot_rows_out[None], own_factor[None], parent[None])


def solution(mesh):
    return jax.shard_map(
        local,
        mesh=mesh,
        in_specs=(
            P(("front", "col"), "row", None),
            P(("front", "col"), "row", None),
            P(("front", "col"), "row", None),
            P(),
        ),
        out_specs=(
            P(("front", "col"), "row", None),
            P(("front", "col"), "row", None),
            P("col", "front", "row"),
        ),
        check_vma=False,
    )
```

profile of v0, /device:TPU:5, one launch (start us, length us, event | category | flops | bytes accessed | tf_op | source)
XLA Modules:
  0.0 1205.6 jit_solution(12534433767830151737)
XLA Ops:
  7.2 1.8 copy.25
  9.1 1.9 copy.27
  11.0 16.4 %all-gather.6.cloned.1.call-done = f32[1,512,512]{1,2,0:T(8,128)} async-done(((f32[1,128,512]{1,2,0:T(8,128)}), f32[1,512,512]{1,2,0:T(8,128)}) %all-gather.6.cloned.1.call-update) | async-done | bytes 1048592 | tf_op jit(solution)/shard_map/all_gather | solution.py:54
  27.5 1.6 copy.26
  29.0 1.4 fusion.23
  30.5 1.0 copy-done.2
  31.5 11.7 cholesky.104
  43.2 9.8 custom-call.31
  53.2 1.2 constant_dynamic-update-slice_fusion.2
  54.4 1.3 convolution_subtract_fusion.2
  55.7 11.7 cholesky.217
  67.4 10.0 custom-call.32
  77.7 1.3 convolution_subtract_fusion.3
  79.0 11.7 cholesky.238
  90.8 0.7 compare_reduce_fusion.1
  91.5 9.8 custom-call.33
  101.5 1.2 convolution_subtract_fusion.4
  102.7 11.7 cholesky.255
  118.3 2.0 fusion.24
  120.3 14.4 %while.1 = (s32[]{:T(128)}, f32[512,512]{1,0:T(8,128)}, s32[4,2]{0,1:T(2,128)S(1)}, f32[4,128,128]{2,1,0:T(8,128)}, s32[]{:T(128)}) while((s32[]{:T(128)}, f32[512,512]{1,0:T(8,128)}, s32[4,2]{0,1:T(2,128)S(1)}, f32[4,128,128]{2,1,0:T(8,128)}, s32[]{:T(128)}) %tuple.46), condition=%wide.while_cond, body=%wide.while_body.sunk | while | flops 2 | bytes 132205 | solution.py:11
  121.0 3.0 bitcast_dynamic-update-slice_fusion.2
  124.6 3.0 bitcast_dynamic-update-slice_fusion.2
  128.2 3.0 bitcast_dynamic-update-slice_fusion.2
  131.8 2.9 bitcast_dynamic-update-slice_fusion.2
  134.7 40.1 %custom-call.34 = f32[4,128,128]{1,2,0:T(8,128)S(1)} custom-call(f32[4,128,128]{2,1,0:T(8,128)} %get-tuple-element.11), custom_call_target="InvertDiagBlocksLowerTriangular" | custom-call | tf_op jit(solution)/shard_map/jit(_solve_triangular)/triangular_solve | solution.py:11
  175.5 1.4 convolution_subtract_fusion.1
  177.6 1.6 convolution_subtract_fusion
  179.8 2.3 fusion.17
  182.7 2.5 fusion.28
  185.7 58.0 %all-gather.4.cloned.1.call-done = f32[4096,512]{0,1:T(8,128)} async-done(((f32[1024,512]{0,1:T(8,128)}), f32[4096,512]{0,1:T(8,128)}) %all-gather.4.cloned.1.call-update) | async-done | bytes 8388624 | tf_op jit(solution)/shard_map/all_gather | solution.py:57
  243.7 30.3 %fusion.7 = f32[128,32,8,128]{3,2,1,0:T(8,128)S(1)} fusion(f32[1,1024,4096]{2,1,0:T(8,128)} %param.8, f32[4096,512]{0,1:T(8,128)} %all-gather.4.cloned.1.call-done, f32[128,1024]{1,0:T(8,128)S(1)} %fusion.37, f32[128,1024]{1,0:T(8,128)S(1)} %fusion.38, f32[128,1024]{1,0:T(8,128)S(1)} %fusion.40, f32[128,1024]{1,0:T(8,128)S(1)} %fusion.25), kind=kOutput, calls=%fused_computation.16 | convolution fusion | flops 25775570944 | bytes 44040192 | tf_op jit(solution)/shard_map/dot_general | solution.py:59
  274.1 6.0 copy.49
  280.1 15.0 %gather_fusion.1 = f32[36,1024,128]{2,1,0:T(8,128)} fusion(f32[1024,32,128]{2,0,1:T(8,128)} %bitcast.119, s32[1024]{0:T(1024)S(1)} %pad_clamp_fusion), kind=kCustom, calls=%fused_computation.3 | custom fusion | bytes 37748880 | tf_op jit(solution)/shard_map/jit(_take)/gather | solution.py:63
  295.0 7.4 select_select_fusion.1
  302.4 208.4 %all_to_all.20 = f32[1024,4,9,128]{3,0,2,1:T(8,128)S(1)} all-to-all(f32[1024,4,9,128]{3,0,2,1:T(8,128)S(1)} %select_select_fusion.1), channel_id=1, replica_groups=mesh['front'=4,'row'=4,'col'=2] {'row'}, dimensions={1} | all-to-all | bytes 37748736 | tf_op jit(solution)/shard_map/all_to_all | solution.py:66
  510.8 6.7 copy.29
  517.5 16.5 %gather_fusion.2 = f32[36,128,9,128]{3,1,2,0:T(8,128)} fusion(f32[32,128,9,128]{3,1,0,2:T(8,128)} %bitcast.117, s32[1024]{0:T(1024)S(1)} %pad_clamp_fusion), kind=kCustom, calls=%fused_computation.4 | custom fusion | bytes 42467472 | tf_op jit(solution)/shard_map/jit(_take)/gather | solution.py:70
  534.0 16.3 %select_select_fusion = f32[4,9,128,9,128]{4,2,3,1,0:T(8,128)} fusion(f32[4,9,128,9,128]{4,2,3,1,0:T(8,128)} %bitcast.118, pred[4,9]{1,0:T(4,128)(4,1)S(1)} %get-tuple-element.61, pred[4,9]{1,0:T(4,128)(4,1)S(1)} %get-tuple-element.60), kind=kLoop, calls=%fused_computation.12 | loop fusion | flops 10616832 | bytes 42467400 | tf_op jit(solution)/shard_map/jit(_where)/select_n | solution.py:72
  550.3 8.1 all-to-all-start.1
  559.5 1.1 gather_fusion.4
  560.6 1.1 gather_fusion.3
  562.1 1.8 copy.33
  564.0 1.7 dynamic-slice_bitcast_fusion
  565.6 450.7 %all-to-all-done.1 = f32[4,9,128,9,128]{4,2,3,1,0:T(8,128)} async-done(((f32[4,9,128,9,128]{4,2,3,1,0:T(8,128)}), f32[4,9,128,9,128]{4,2,3,1,0:T(8,128)}, u32[]{:S(2)}, u32[]{:S(2)}) %all-to-all-start.1) | async-done | bytes 21233696 | tf_op jit(solution)/shard_map/all_to_all | solution.py:73
  1016.3 40.1 %fusion.4 = f32[4,9,128,24,128]{4,3,2,1,0:T(8,128)} fusion(f32[4,9,128,9,128]{4,2,3,1,0:T(8,128)} %all-to-all-done.1, s32[4,9]{1,0:T(4,128)S(1)} %select_subtract_fusion, pred[4,9]{1,0:T(4,128)(4,1)S(1)} %get-tuple-element.64), kind=kOutput, calls=%fused_computation.11 | convolution fusion | flops 1528825600 | bytes 77856944 | tf_op jit(solution)/shard_map/fsxty,fbt->fsxby/dot_general | solution.py:78
  1056.4 68.6 %fusion.8 = f32[24,128,24,128]{3,0,2,1:T(8,128)} fusion(f32[4,9,128,24,128]{4,3,2,1,0:T(8,128)} %fusion.4, pred[4,24,9,1,1]{1,2,0,4,3:T(8,128)(4,1)S(1)} %fusion.76), kind=kOutput, calls=%fused_computation.17 | convolution fusion | flops 4076863488 | bytes 94372704 | tf_op jit(solution)/shard_map/fas,fsxby->axby/dot_general | solution.py:79
  1125.1 33.1 %copy.32 = f32[24,128,24,128]{3,2,1,0:T(8,128)} copy(f32[24,128,24,128]{3,0,2,1:T(8,128)} %fusion.8) | data formatting | bytes 75497472 | tf_op jit(solution)/shard_map/fas,fsxby->axby/dot_general | solution.py:79
  1158.1 40.2 %broadcast_in_dim_reshape.3 = f32[1,3072,3072]{2,1,0:T(8,128)} reshape(f32[24,128,24,128]{3,2,1,0:T(8,128)} %copy.32) | data formatting | bytes 75497472 | tf_op jit(solution)/shard_map/broadcast_in_dim;reshape | solution.py:82
  (60 shorter events, 9.3 us)
Async XLA Ops:
  7.2 20.3 %all-gather.6.cloned.1.call-start = ((), (), s32[]{:S(2)}) async-start(), calls=%async_computation.3 | async-start | bytes 1310720 | tf_op jit(solution)/shard_map/all_gather | solution.py:54
  9.0 234.7 %all-gather.4.cloned.1.call-start = ((), (), s32[]{:S(2)}) async-start(), calls=%async_computation.2 | async-start | bytes 10485760 | tf_op jit(solution)/shard_map/all_gather | solution.py:57
  11.0 166.5 %copy-start.1 = (f32[1,1024,512]{1,2,0:T(8,128)}, f32[1,1024,512]{1,2,0:T(8,128)S(1)}, u32[]{:S(2)}) copy-start(f32[1,1024,512]{1,2,0:T(8,128)S(1)} %copy.27) | copy-start | bytes 6291460
  27.5 157.8 %copy-start.3 = (s32[8,32]{1,0:T(8,128)S(1)}, s32[8,32]{1,0:T(8,128)}, u32[]{:S(2)}) copy-start(s32[8,32]{1,0:T(8,128)} %param.9) | copy-start | bytes 3076
  30.5 1.0 copy-start.2
  550.3 11.8 copy-start
  550.3 466.0 %all-to-all-start.1 = ((f32[4,9,128,9,128]{4,2,3,1,0:T(8,128)}), f32[4,9,128,9,128]{4,2,3,1,0:T(8,128)}, u32[]{:S(2)}, u32[]{:S(2)}) async-start(f32[4,9,128,9,128]{4,2,3,1,0:T(8,128)} %select_select_fusion), calls=%async_computation.1 | async-start | bytes 42467328 | tf_op jit(solution)/shard_map/all_to_all | solution.py:73
Sparse Core Ops, SparseCore 0:
  10.1 17.2 all-gather.5
  185.4 58.2 all-gather.3
where the time goes:
time: 1220 us; the launch traced here: 1210 us
  waiting for transfers between devices  525 us (43%)
  blocking collectives  208 us (17%)
  matrix products  152 us (12%)
  other arithmetic  149 us (12%)
  local copies, waits for them, and re-layouts  145 us (12%)
  between operations  17.3 us (1%)
    all_to_all x1, waiting for transfers between devices, local(): lax.all_to_all(picked, 'front', split_axis=0, concat_axis=0, tiled=True)  451 us
    all_to_all x1, blocking collectives, local(): lax.all_to_all(source, 'row', split_axis=1, concat_axis=0, tiled=True)  208 us
    another operation x14, other arithmetic, local(): lower_factor = jnp.linalg.cholesky(pivot_whole)  78.6 us
    dot_general x1, matrix products, local(): jnp.einsum('fas,fsxby->axby', row_hot, partial_value, precision=lax.Preci...  68.6 us
    all_gather x1, waiting for transfers between devices, local(): all_factor = lax.all_gather(own_factor, 'row', axis=0, tiled=True)  58 us
    another operation x3, other arithmetic, solve_panel(): jax.scipy.linalg.solve_triangular(lower_factor, panel_block.T, lower=True)  42.1 us
    another operation x1, local copies, waits for them, and re-layouts, local(): return (pivot_rows_out[None], own_factor[None], parent[None])  40.2 us
    dot_general x1, matrix products, local(): jnp.einsum('fsxty,fbt->fsxby', routed, col_hot, precision=lax.Precision.H...  40.1 us
  transfers between devices with their start and end apart: 3, of which 3 were waited for; matrix products, arithmetic and copies ran while one was open for 1% of the time, Pallas kernels for 0%

commit v1 on v0

v1 whole, which is shorter than its diff:
```python
import functools

import jax
import jax.numpy as jnp
from jax import lax
from jax.experimental import pallas as pl
from jax.experimental.pallas import tpu as pltpu
from jax.sharding import PartitionSpec as P

TILE = 128
PARENT = 12288
GROUP = 4
HIGHEST = lax.Precision.HIGHEST
NT = (((1,), (1,)), ((), ()))
NN = (((1,), (0,)), ((), ()))


def mul(left, right, dims):
    return lax.dot_general(left, right, dims, precision=HIGHEST, preferred_element_type=jnp.float32)


def factor_tile(block):
    size = block.shape[0]
    row_ids = lax.broadcasted_iota(jnp.int32, (size, size), 0)
    col_ids = lax.broadcasted_iota(jnp.int32, (size, size), 1)
    inverse = (row_ids == col_ids).astype(jnp.float32)
    work = block
    scales = jnp.zeros((size, size), jnp.float32)
    for first in range(0, size, GROUP):
        base = first // 8 * 8
        tail = work[base:, :]
        tail_inverse = inverse[base:, :]
        rows_here = row_ids[base:, :]
        columns = [
            jnp.broadcast_to(tail[:, k : k + 1], tail.shape) for k in range(first, first + GROUP)
        ]
        for offset in range(GROUP):
            k = first + offset
            at = k - base
            column = columns[offset]
            pivot = column[at : at + 1, :]
            recip = 1.0 / pivot
            multiplier = jnp.where(rows_here > k, column * recip, 0.0)
            for later in range(offset + 1, GROUP):
                columns[later] = columns[later] - multiplier * columns[later][at : at + 1, :]
            tail_inverse = tail_inverse - multiplier * tail_inverse[at : at + 1, :]
            tail = tail - multiplier * tail[at : at + 1, :]
            scales = jnp.where(row_ids == k, lax.rsqrt(pivot), scales)
        if base:
            work = jnp.concatenate([work[:base, :], tail], axis=0)
            inverse = jnp.concatenate([inverse[:base, :], tail_inverse], axis=0)
        else:
            work, inverse = tail, tail_inverse
    upper = jnp.where(col_ids >= row_ids, work * scales, 0.0)
    return upper.T, inverse * scales


def pivot_kernel(pivot_ref, lower_ref, inverse_ref, work):
    size = pivot_ref.shape[0]
    blocks = size // TILE
    lower_ref[...] = jnp.zeros_like(lower_ref)
    inverse_ref[...] = jnp.zeros_like(inverse_ref)
    work[...] = pivot_ref[...]

    @pl.loop(0, blocks)
    def _(step):
        at = pl.ds(pl.multiple_of(step * TILE, TILE), TILE)
        lower, inverse = factor_tile(work[at, at])
        rows = lax.broadcasted_iota(jnp.int32, (size, TILE), 0)
        below = mul(work[:, at], inverse, NT)
        below = jnp.where(rows >= (step + 1) * TILE, below, 0.0)
        work[...] = work[...] - mul(below, below, NT)
        lower_ref[:, at] = below
        lower_ref[at, at] = lower
        inverse_ref[at, at] = inverse

    for block in range(1, blocks):
        lo, hi = block * TILE, (block + 1) * TILE
        partial = mul(lower_ref[lo:hi, :lo], inverse_ref[:lo, :lo], NN)
        inverse_ref[lo:hi, :lo] = -mul(inverse_ref[lo:hi, lo:hi], partial, NN)


def factor_pivot(pivot):
    size = pivot.shape[0]
    whole = pl.BlockSpec(memory_space=pltpu.VMEM)
    return pl.pallas_call(
        pivot_kernel,
        out_shape=[jax.ShapeDtypeStruct((size, size), jnp.float32)] * 2,
        in_specs=[whole],
        out_specs=[whole, whole],
        scratch_shapes=[pltpu.VMEM((size, size), jnp.float32)],
        compiler_params=pltpu.CompilerParams(vmem_limit_bytes=32 * 2**20),
        cost_estimate=pl.CostEstimate(flops=60 * 10**9, bytes_accessed=3 * 2**20, transcendentals=0),
        name="factor_pivot",
    )(pivot)


def split(value):
    high = value.astype(jnp.bfloat16)
    return high, (value - high.astype(jnp.float32)).astype(jnp.bfloat16)


def contribution_kernel(
    own_tiles, left_tiles, chunk, info, panel, own, halo, out, update, mine_high, mine_low, high, low, sems
):
    fronts = update.shape[0]
    width = update.shape[2]
    slots = width // TILE
    step = pl.program_id(0)
    mine_first = info[fronts]
    row_me = info[fronts + 1]

    @pl.when(step == 0)
    def _():
        for f in range(fronts):
            columns = pl.ds(pl.multiple_of(info[f] * TILE, TILE), width)
            for slot in range(slots):
                place = mine_first + slot - own_tiles * row_me
                inside = (place >= 0) & (place < own_tiles)
                target = update.at[f, pl.ds(slot * TILE, TILE), :]

                @pl.when(inside)
                def _():
                    rows = pl.ds(pl.multiple_of(place * TILE, TILE), TILE)
                    pltpu.make_async_copy(own.at[rows, columns], target, sems.at[f]).start()

                @pl.when(jnp.logical_not(inside))
                def _():
                    which = jnp.where(place < 0, -place - 1, left_tiles + place - own_tiles)
                    rows = pl.ds(pl.multiple_of(which * TILE, TILE), TILE)
                    pltpu.make_async_copy(halo.at[rows, columns], target, sems.at[f]).start()

        value = panel[pl.ds(pl.multiple_of(mine_first * TILE, TILE), width), :]
        mine_high[...], mine_low[...] = split(value)

    value = panel[pl.ds(pl.multiple_of(info[step] * TILE, TILE), width), :]
    high[...], low[...] = split(value)
    pltpu.make_async_copy(update.at[step], update.at[step], sems.at[step]).wait()

    def dot(left, right):
        return lax.dot_general(left, right, NT, preferred_element_type=jnp.float32)

    @pl.loop(0, slots // chunk)
    def _(part):
        at = pl.ds(pl.multiple_of(part * chunk * TILE, TILE), chunk * TILE)
        product = dot(high[...], mine_low[at, :]) + dot(low[...], mine_high[at, :])
        product = product + dot(high[...], mine_high[at, :])
        out[0, :, at] = update[step, at, :].T - product


def contribute(panel, own, halo, info, fronts, slots, own_tiles, left_tiles):
    width = slots * TILE
    depth = panel.shape[1]
    chunk = 3 if slots % 3 == 0 else 1
    return pl.pallas_call(
        functools.partial(contribution_kernel, own_tiles, left_tiles, chunk),
        out_shape=jax.ShapeDtypeStruct((fronts, width, width), jnp.float32),
        grid_spec=pltpu.PrefetchScalarGridSpec(
            num_scalar_prefetch=1,
            grid=(fronts,),
            in_specs=[
                pl.BlockSpec(memory_space=pltpu.VMEM),
                pl.BlockSpec(memory_space=pl.ANY),
                pl.BlockSpec(memory_space=pl.ANY),
            ],
            out_specs=pl.BlockSpec((1, width, width), lambda f, info: (f, 0, 0)),
            scratch_shapes=[
                pltpu.VMEM((fronts, width, width), jnp.float32),
                pltpu.VMEM((width, depth), jnp.bfloat16),
                pltpu.VMEM((width, depth), jnp.bfloat16),
                pltpu.VMEM((width, depth), jnp.bfloat16),
                pltpu.VMEM((width, depth), jnp.bfloat16),
                pltpu.SemaphoreType.DMA((fronts,)),
            ],
        ),
        compiler_params=pltpu.CompilerParams(vmem_limit_bytes=60 * 2**20),
        cost_estimate=pl.CostEstimate(
            flops=6 * fronts * width * width * depth, bytes_accessed=8 * fronts * width * width, transcendentals=0
        ),
        name="contribute",
    )(info, panel, own, halo)


def assemble_kernel(fronts, slots, fetch, valid, target, *refs):
    blocks, out = refs[:fronts], refs[fronts]
    here = pl.program_id(0)
    out[...] = jnp.zeros_like(out)
    for k in range(fronts):

        @pl.when(valid[k, here] > 0)
        def _():
            for slot in range(slots):
                place = target[k, slot]

                @pl.when(place >= 0)
                def _():
                    at = pl.ds(pl.multiple_of(place * TILE, TILE), TILE)
                    out[:, at] = out[:, at] + blocks[k][0, :, slot * TILE : (slot + 1) * TILE]


def assemble(routed, fetch, valid, target, block_width):
    fronts, width, _ = routed.shape
    slots = width // TILE
    order = block_width * TILE

    def spec(k):
        return pl.BlockSpec((1, TILE, width), lambda a, fetch, valid, target: (k, fetch[k, a], 0))

    return pl.pallas_call(
        functools.partial(assemble_kernel, fronts, slots),
        out_shape=jax.ShapeDtypeStruct((order, order), jnp.float32),
        grid_spec=pltpu.PrefetchScalarGridSpec(
            num_scalar_prefetch=3,
            grid=(block_width,),
            in_specs=[spec(k) for k in range(fronts)],
            out_specs=pl.BlockSpec((TILE, order), lambda a, fetch, valid, target: (a, 0)),
        ),
        compiler_params=pltpu.CompilerParams(vmem_limit_bytes=48 * 2**20),
        cost_estimate=pl.CostEstimate(
            flops=0, bytes_accessed=4 * (fronts * width * width + order * order), transcendentals=0
        ),
        name="assemble",
    )(fetch, valid, target, *([routed] * fronts))


def exchange_halo(own, row_count, own_tiles, slots, tiles):
    left, right = [], []
    for r in range(row_count):
        left.append(own_tiles * r - max(0, tiles - slots * (row_count - r)))
        right.append(min(tiles, slots * (r + 1)) - own_tiles * (r + 1))

    def tile_row(index):
        return lax.slice_in_dim(own, index * TILE, (index + 1) * TILE, axis=0)

    pieces = []
    for t in range(1, max(left) + 1):
        distance = (t + own_tiles - 1) // own_tiles
        pairs = [(r - distance, r) for r in range(row_count) if left[r] >= t]
        pieces.append(lax.ppermute(tile_row(-t % own_tiles), "row", pairs))
    for t in range(max(right)):
        distance = 1 + t // own_tiles
        pairs = [(r + distance, r) for r in range(row_count) if right[r] > t]
        pieces.append(lax.ppermute(tile_row(t % own_tiles), "row", pairs))
    return jnp.concatenate(pieces, axis=0), max(left)


def local(pivot_block, panel_rows, update_block, tile_map):
    row_count = lax.axis_size("row")
    front_count = lax.axis_size("front")
    col_count = lax.axis_size("col")
    row_me = lax.axis_index("row")
    front_me = lax.axis_index("front")
    col_me = lax.axis_index("col")
    pivot_share = pivot_block.shape[1]
    own_rows = panel_rows.shape[1]
    tiles = update_block.shape[2] // TILE
    own_tiles = own_rows // TILE
    row_width = PARENT // TILE // row_count
    slots = tiles // row_count + 1

    pivot_whole = lax.all_gather(pivot_block[0], "row", axis=0, tiled=True)
    panel_whole = lax.all_gather(panel_rows[0], "row", axis=0, tiled=True)
    halo, left_tiles = exchange_halo(update_block[0], row_count, own_tiles, slots, tiles)

    def first_tile(maps, block):
        count = jnp.sum((maps // row_width < block).astype(jnp.int32), axis=-1)
        return jnp.minimum(count, tiles - slots)

    child_map = lax.dynamic_index_in_dim(tile_map, front_me * col_count + col_me, 0, keepdims=False)
    block_ids = jnp.arange(front_count, dtype=jnp.int32)
    info = jnp.concatenate(
        [
            first_tile(child_map[None, :], block_ids[:, None]),
            jnp.stack([first_tile(child_map, row_me), row_me]).astype(jnp.int32),
        ]
    )
    sources = jnp.arange(front_count, dtype=jnp.int32) * col_count + col_me
    maps = jnp.take(tile_map, sources, axis=0)
    slot_ids = jnp.arange(slots, dtype=jnp.int32)[None, :]
    row_first = first_tile(maps, front_me)[:, None]
    picked = jnp.take_along_axis(maps, row_first + slot_ids, axis=1) - front_me * row_width
    places = jnp.arange(row_width, dtype=jnp.int32)
    hit = picked[:, :, None] == places[None, None, :]
    valid = jnp.any(hit, axis=1).astype(jnp.int32)
    reached = jnp.sum((picked[:, :, None] <= places[None, None, :]).astype(jnp.int32), axis=1)
    fetch = jnp.clip(reached - 1, 0, slots - 1)
    col_first = first_tile(maps, row_me)[:, None]
    target = jnp.take_along_axis(maps, col_first + slot_ids, axis=1) - row_me * row_width
    target = jnp.where((target >= 0) & (target < row_width), target, -1)

    lower, inverse = factor_pivot(pivot_whole)
    panel = mul(panel_whole, inverse, NT)
    source = contribute(
        panel, update_block[0], halo, info, front_count, slots, own_tiles, left_tiles
    )
    routed = lax.all_to_all(source, "front", split_axis=0, concat_axis=0, tiled=True)
    parent = assemble(routed, fetch, valid, target, row_width)
    lower_own = lax.dynamic_slice_in_dim(lower, row_me * pivot_share, pivot_share, 0)
    panel_own = lax.dynamic_slice_in_dim(panel, row_me * own_rows, own_rows, 0)
    return (lower_own[None], panel_own[None], parent[None])


def solution(mesh):
    return jax.shard_map(
        local,
        mesh=mesh,
        in_specs=(
            P(("front", "col"), "row", None),
            P(("front", "col"), "row", None),
            P(("front", "col"), "row", None),
            P(),
        ),
        out_specs=(
            P(("front", "col"), "row", None),
            P(("front", "col"), "row", None),
            P("col", "front", "row"),
        ),
        check_vma=False,
    )
```

time: 1220 us -> 694 us (0.57); the launches traced: 1210 us -> 693 us
  blocking collectives: 208 us -> 0 us
  other arithmetic: 149 us -> 2.26 us
  matrix products: 152 us -> 17.2 us
  local copies, waits for them, and re-layouts: 145 us -> 34.7 us
  Pallas kernels: 0 us -> 97.5 us
  waiting for transfers between devices: 525 us -> 452 us
  starting transfers between devices: 8.16 us -> 74.8 us
    all_to_all x1 -> x0, blocking collectives: 208 us -> none  [local(): lax.all_to_all(source, 'row', split_axis=1, concat_axis=0, tiled=True)]
    dot_general x3 -> x1, matrix products: 139 us -> 17.2 us  [mul(): lax.dot_general(left, right, dims, precision=HIGHEST, preferred_element_t...]
    another operation x17 -> x0, other arithmetic: 121 us -> none  [the longest x14 78.6 us: local(): lower_factor = jnp.linalg.cholesky(pivot_whole)]
    pallas_call x0 -> x3, Pallas kernels: none -> 97.5 us  [the longest x1 34.4 us: contribute(): pl.pallas_call(functools.partial(contribution_kernel, own_tiles, left_til...]
    ppermute x0 -> x6, starting transfers between devices: none -> 67 us  [the longest x3 61.7 us: exchange_halo(): pieces.append(lax.ppermute(tile_row(t % own_tiles), 'row', pairs))]
    all_gather x1, waiting for transfers between devices: 58 us -> 0.01 us  [local(): panel_whole = lax.all_gather(panel_rows[0], 'row', axis=0, tiled=True)]
    another operation x18 -> x0, local copies, waits for them, and re-layouts: 54.8 us -> none  [the longest x1 40.2 us: local(): return (pivot_rows_out[None], own_factor[None], parent[None])]
    dot_general x1 -> x0, local copies, waits for them, and re-layouts: 33.1 us -> none  [local(): jnp.einsum('fas,fsxby->axby', row_hot, partial_value, precision=lax.Preci...]
  transfers between devices with their start and end apart: 3 -> 9, of which waited for: 3 -> 1; matrix products, arithmetic and copies ran while one was open for 1% -> 5% of each run, Pallas kernels for 0% -> 5%
where the time goes in v1:
time: 694 us; the launch traced here: 693 us
  waiting for transfers between devices  452 us (65%)
  Pallas kernels  97.5 us (14%)
  starting transfers between devices  74.8 us (11%)
  local copies, waits for them, and re-layouts  34.7 us (5%)
  matrix products  17.2 us (2%)
  between operations  14.8 us (2%)
    all_to_all x1, waiting for transfers between devices, local(): lax.all_to_all(source, 'front', split_axis=0, concat_axis=0, tiled=True)  451 us
    ppermute x3, starting transfers between devices, exchange_halo(): pieces.append(lax.ppermute(tile_row(t % own_tiles), 'row', pairs))  61.7 us
    pallas_call x1, Pallas kernels, contribute(): pl.pallas_call(functools.partial(contribution_kernel, own_tiles, left_til...  34.4 us
    pallas_call x1, Pallas kernels, assemble(): pl.pallas_call(functools.partial(assemble_kernel, fronts, slots), out_sha...  31.6 us
    pallas_call x1, Pallas kernels, factor_pivot(): pl.pallas_call(pivot_kernel, out_shape=[jax.ShapeDtypeStruct((size, size)...  31.4 us
    dot_general x1, matrix products, mul(): lax.dot_general(left, right, dims, precision=HIGHEST, preferred_element_t...  17.2 us
    unnamed x11, local copies, waits for them, and re-layouts  16.8 us
  transfers between devices with their start and end apart: 9, of which 1 were waited for; matrix products, arithmetic and copies ran while one was open for 5% of the time, Pallas kernels for 5%

profile of v1, /device:TPU:5, one launch (start us, length us, event | category | flops | bytes accessed | tf_op | source)
XLA Modules:
  0.0 693.3 jit_solution(13307052607958569561)
XLA Ops:
  7.2 0.0 all-gather.5.cloned.1.call-start
  7.2 0.7 all-gather.5.cloned.1.call-update
  7.9 0.0 all-gather.7.cloned.1.call-start
  7.9 0.7 all-gather.7.cloned.1.call-update
  8.7 9.5 %slice_bitcast_fusion = (f32[128,4096]{1,0:T(8,128)}, f32[128,4096]{1,0:T(8,128)}, f32[128,4096]{1,0:T(8,128)}, f32[128,4096]{1,0:T(8,128)}, f32[128,4096]{1,0:T(8,128)}, /*index=5*/f32[128,4096]{1,0:T(8,128)}) fusion(f32[1,1024,4096]{2,1,0:T(8,128)} %param.8), kind=kLoop, calls=%fused_computation.5 | loop fusion | bytes 25165824 | tf_op jit(solution)/shard_map/slice | solution.py:233
  18.1 3.9 collective-permute-start.3
  22.0 2.0 collective-permute-start.2
  24.0 2.0 collective-permute-start.1
  26.0 1.3 collective-permute-start
  27.3 4.4 collective-permute-start.4
  31.7 0.7 fusion.11
  33.1 0.1 convert_reduce_fusion.1
  33.2 0.7 pad_add_fusion.info
  33.9 1.2 copy-done
  35.1 31.4 %factor_pivot.1 = (f32[512,512]{1,0:T(8,128)S(1)}, f32[512,512]{1,0:T(8,128)S(1)}) custom-call(f32[512,512]{1,0:T(8,128)S(1)} %bitcast.43), custom_call_target="tpu_custom_call" | custom-call | flops 60000002048 | bytes 3145728 | tf_op jit(solution)/shard_map/factor_pivot/pallas_call | solution.py:86
  66.5 0.0 collective-permute-done
  66.6 53.4 %collective-permute-start.5 = (f32[128,4096]{1,0:T(8,128)S(1)}, f32[128,4096]{1,0:T(8,128)S(1)}, u32[]{:S(2)}, u32[]{:S(2)}) collective-permute-start(f32[128,4096]{1,0:T(8,128)S(1)} %copy-done.1), channel_id=1, source_target_pairs={{6,4},{7,5},{14,12},{15,13},{22,20},{23,21},{30,28},{31,29}} | collective-permute-start | bytes 6291464 | tf_op jit(solution)/shard_map/ppermute | solution.py:243
  120.0 3.1 constant_dynamic-update-slice_fusion.5
  123.1 3.1 constant_dynamic-update-slice_fusion.4
  126.2 3.1 constant_dynamic-update-slice_fusion.3
  129.4 3.1 constant_dynamic-update-slice_fusion.2
  132.5 0.0 collective-permute-done.4
  132.5 3.1 constant_dynamic-update-slice_fusion.1
  135.6 0.0 collective-permute-done.5
  135.6 1.5 constant_dynamic-update-slice_fusion.halo
  137.1 17.2 %fusion.panel = f32[4096,512]{1,0:T(8,128)} fusion(f32[512,512]{1,0:T(8,128)S(1)} %get-tuple-element.7, f32[1,4096,512]{2,1,0:T(8,128)} %all-gather.7.cloned.1.call-done), kind=kOutput, calls=%fused_computation.3 | convolution fusion | flops 12884901888 | bytes 17825792 | tf_op jit(solution)/shard_map/dot_general | solution.py:19
  154.3 34.4 %contribute.1 = f32[4,1152,1152]{2,1,0:T(8,128)} custom-call(s32[6]{0:T(128)} %pad_add_fusion.info, f32[4096,512]{1,0:T(8,128)} %fusion.panel, f32[1024,4096]{1,0:T(8,128)} %bitcast.45, f32[768,4096]{1,0:T(8,128)} %constant_dynamic-update-slice_fusion.halo), custom_call_target="tpu_custom_call" | custom-call | flops 16307453952 | bytes 42467328 | tf_op jit(solution)/shard_map/contribute/pallas_call | solution.py:155
  188.8 7.8 %all-to-all-start = ((f32[4,1152,1152]{2,1,0:T(8,128)}), f32[4,1152,1152]{2,1,0:T(8,128)}, u32[]{:S(2)}, u32[]{:S(2)}) async-start(f32[4,1152,1152]{2,1,0:T(8,128)} %contribute.1), calls=%async_computation | async-start | bytes 42467328 | tf_op jit(solution)/shard_map/all_to_all | solution.py:296
  196.5 0.6 gather_fusion
  197.1 0.1 add_select_fusion
  197.2 0.1 convert_reduce_fusion.2
  197.4 0.1 bitcast_or_fusion.1
  197.4 0.1 reshape.95
  197.5 1.1 gather_fusion.1
  198.6 0.1 reshape.98
  198.7 0.1 bitcast_or_fusion
  198.8 0.1 reshape.100
  198.8 1.1 gather_fusion.2
  199.9 0.1 reshape.103
  200.0 0.1 select_subtract_fusion.1
  200.1 0.1 copy.7
  200.2 0.1 fusion.2
  200.3 0.1 convert_reduce_fusion
  200.4 0.1 and_select_fusion.target
  200.5 0.7 dynamic-slice_bitcast_fusion.1
  201.2 3.1 dynamic-slice_bitcast_fusion
  204.3 450.6 %all-to-all-done.refs_0_.refs_1_.refs_2_.refs_3_ = f32[4,1152,1152]{2,1,0:T(8,128)} async-done(((f32[4,1152,1152]{2,1,0:T(8,128)}), f32[4,1152,1152]{2,1,0:T(8,128)}, u32[]{:S(2)}, u32[]{:S(2)}) %all-to-all-start) | async-done | bytes 21233696 | tf_op jit(solution)/shard_map/all_to_all | solution.py:296
  654.8 31.6 %assemble.1 = f32[3072,3072]{1,0:T(8,128)} custom-call(s32[4,24]{1,0:T(4,128)S(1)} %add_clamp_fusion.fetch, s32[4,24]{1,0:T(4,128)S(1)} %convert_element_type.20.valid, s32[4,9]{1,0:T(4,128)S(1)} %and_select_fusion.target, f32[4,1152,1152]{2,1,0:T(8,128)} %all-to-all-done.refs_0_.refs_1_.refs_2_.refs_3_, ...), custom_call_target="tpu_custom_call" | custom-call | bytes 58982400 | tf_op jit(solution)/shard_map/assemble/pallas_call | solution.py:209
  (19 shorter events, 0.1 us)
Async XLA Ops:
  7.2 26.7 %all-gather.5.cloned.1.call-start = ((), (), s32[]{:S(2)}) async-start(), calls=%async_computation.1 | async-start | bytes 1310720 | tf_op jit(solution)/shard_map/all_gather | solution.py:261
  7.9 129.2 %all-gather.7.cloned.1.call-start = ((), (), s32[]{:S(2)}) async-start(), calls=%async_computation.2 | async-start | bytes 10485760 | tf_op jit(solution)/shard_map/all_gather | solution.py:262
  8.6 23.1 %copy-start.2 = (s32[8,32]{1,0:T(8,128)S(1)}, s32[8,32]{1,0:T(8,128)}, u32[]{:S(2)}) copy-start(s32[8,32]{1,0:T(8,128)} %param.9) | copy-start | bytes 3076
  18.1 111.2 %collective-permute-start.3 = (f32[128,4096]{1,0:T(8,128)}, f32[128,4096]{1,0:T(8,128)}, u32[]{:S(2)}, u32[]{:S(2)}) collective-permute-start(f32[128,4096]{1,0:T(8,128)} %get-tuple-element.15), channel_id=1, source_target_pairs={{2,0},{4,2},{6,4},{3,1},{5,3},{7,5},{10,8},{12,10},{14,12},{11,9},... | collective-permute-start | bytes 6291464 | tf_op jit(solution)/shard_map/ppermute | solution.py:243
  22.0 104.2 %collective-permute-start.2 = (f32[128,4096]{1,0:T(8,128)}, f32[128,4096]{1,0:T(8,128)}, u32[]{:S(2)}, u32[]{:S(2)}) collective-permute-start(f32[128,4096]{1,0:T(8,128)} %get-tuple-element.16), channel_id=1, source_target_pairs={{0,2},{1,3},{8,10},{9,11},{16,18},{17,19},{24,26},{25,27}} | collective-permute-start | bytes 6291464 | tf_op jit(solution)/shard_map/ppermute | solution.py:239
  24.0 99.1 %collective-permute-start.1 = (f32[128,4096]{1,0:T(8,128)}, f32[128,4096]{1,0:T(8,128)}, u32[]{:S(2)}, u32[]{:S(2)}) collective-permute-start(f32[128,4096]{1,0:T(8,128)} %get-tuple-element.17), channel_id=1, source_target_pairs={{0,2},{2,4},{1,3},{3,5},{8,10},{10,12},{9,11},{11,13},{16,18},{18,... | collective-permute-start | bytes 6291464 | tf_op jit(solution)/shard_map/ppermute | solution.py:239
  26.0 40.5 %collective-permute-start = (f32[128,4096]{1,0:T(8,128)}, f32[128,4096]{1,0:T(8,128)}, u32[]{:S(2)}, u32[]{:S(2)}) collective-permute-start(f32[128,4096]{1,0:T(8,128)} %get-tuple-element.18), channel_id=1, source_target_pairs={{0,2},{2,4},{4,6},{1,3},{3,5},{5,7},{8,10},{10,12},{12,14},{9,11},... | collective-permute-start | bytes 6291464 | tf_op jit(solution)/shard_map/ppermute | solution.py:239
  27.3 105.2 %collective-permute-start.4 = (f32[128,4096]{1,0:T(8,128)}, f32[128,4096]{1,0:T(8,128)}, u32[]{:S(2)}, u32[]{:S(2)}) collective-permute-start(f32[128,4096]{1,0:T(8,128)} %get-tuple-element.19), channel_id=1, source_target_pairs={{4,2},{6,4},{5,3},{7,5},{12,10},{14,12},{13,11},{15,13},{20,18},{2... | collective-permute-start | bytes 6291464 | tf_op jit(solution)/shard_map/ppermute | solution.py:243
  33.9 1.2 copy-start
  35.1 31.4 %copy-start.1 = (f32[128,4096]{1,0:T(8,128)S(1)}, f32[128,4096]{1,0:T(8,128)}, u32[]{:S(2)}) copy-start(f32[128,4096]{1,0:T(8,128)} %get-tuple-element.14) | copy-start | bytes 6291460
  66.6 69.1 %collective-permute-start.5 = (f32[128,4096]{1,0:T(8,128)S(1)}, f32[128,4096]{1,0:T(8,128)S(1)}, u32[]{:S(2)}, u32[]{:S(2)}) collective-permute-start(f32[128,4096]{1,0:T(8,128)S(1)} %copy-done.1), channel_id=1, source_target_pairs={{6,4},{7,5},{14,12},{15,13},{22,20},{23,21},{30,28},{31,29}} | collective-permute-start | bytes 6291464 | tf_op jit(solution)/shard_map/ppermute | solution.py:243
  188.8 466.1 %all-to-all-start = ((f32[4,1152,1152]{2,1,0:T(8,128)}), f32[4,1152,1152]{2,1,0:T(8,128)}, u32[]{:S(2)}, u32[]{:S(2)}) async-start(f32[4,1152,1152]{2,1,0:T(8,128)} %contribute.1), calls=%async_computation | async-start | bytes 42467328 | tf_op jit(solution)/shard_map/all_to_all | solution.py:296
Sparse Core Ops, SparseCore 0:
  9.6 17.1 all-gather.4
  28.3 83.3 all-gather.6

commit v2 on v1

--- a/solution.py
+++ b/solution.py
@@ -100,37 +100,34 @@
     return high, (value - high.astype(jnp.float32)).astype(jnp.bfloat16)
 
 
-def contribution_kernel(
-    own_tiles, left_tiles, chunk, info, panel, own, halo, out, update, mine_high, mine_low, high, low, sems
-):
-    fronts = update.shape[0]
-    width = update.shape[2]
-    slots = width // TILE
+def contribution_kernel(own_tiles, left_tiles, first_slot, pieces, info, panel, own, *refs):
+    halo, (out, update, mine_high, mine_low, high, low, sems) = refs[:pieces], refs[-7:]
+    fronts, mine_width, width = update.shape
     step = pl.program_id(0)
-    mine_first = info[fronts]
+    mine_first = info[fronts] + first_slot
     row_me = info[fronts + 1]
 
     @pl.when(step == 0)
     def _():
         for f in range(fronts):
             columns = pl.ds(pl.multiple_of(info[f] * TILE, TILE), width)
-            for slot in range(slots):
+            for slot in range(mine_width // TILE):
                 place = mine_first + slot - own_tiles * row_me
-                inside = (place >= 0) & (place < own_tiles)
                 target = update.at[f, pl.ds(slot * TILE, TILE), :]
 
-                @pl.when(inside)
+                @pl.when((place >= 0) & (place < own_tiles))
                 def _():
                     rows = pl.ds(pl.multiple_of(place * TILE, TILE), TILE)
                     pltpu.make_async_copy(own.at[rows, columns], target, sems.at[f]).start()
 
-                @pl.when(jnp.logical_not(inside))
-                def _():
-                    which = jnp.where(place < 0, -place - 1, left_tiles + place - own_tiles)
-                    rows = pl.ds(pl.multiple_of(which * TILE, TILE), TILE)
-                    pltpu.make_async_copy(halo.at[rows, columns], target, sems.at[f]).start()
-
-        value = panel[pl.ds(pl.multiple_of(mine_first * TILE, TILE), width), :]
+                for piece in range(pieces):
+                    at = -piece - 1 if piece < left_tiles else own_tiles + piece - left_tiles
+
+                    @pl.when(place == at)
+                    def _():
+                        pltpu.make_async_copy(halo[piece].at[:, columns], target, sems.at[f]).start()
+
+        value = panel[pl.ds(pl.multiple_of(mine_first * TILE, TILE), mine_width), :]
         mine_high[...], mine_low[...] = split(value)
 
     value = panel[pl.ds(pl.multiple_of(info[step] * TILE, TILE), width), :]
@@ -140,79 +137,76 @@
     def dot(left, right):
         return lax.dot_general(left, right, NT, preferred_element_type=jnp.float32)
 
-    @pl.loop(0, slots // chunk)
-    def _(part):
-        at = pl.ds(pl.multiple_of(part * chunk * TILE, TILE), chunk * TILE)
-        product = dot(high[...], mine_low[at, :]) + dot(low[...], mine_high[at, :])
-        product = product + dot(high[...], mine_high[at, :])
-        out[0, :, at] = update[step, at, :].T - product
-
-
-def contribute(panel, own, halo, info, fronts, slots, own_tiles, left_tiles):
+    product = dot(high[...], mine_low[...]) + dot(low[...], mine_high[...])
+    product = product + dot(high[...], mine_high[...])
+    out[0] = update[step].T - product
+
+
+def contribute(panel, own, halo, after, info, fronts, slots, first_slot, chunk, own_tiles, left_tiles):
     width = slots * TILE
+    mine_width = chunk * TILE
     depth = panel.shape[1]
-    chunk = 3 if slots % 3 == 0 else 1
+    anywhere = pl.BlockSpec(memory_space=pl.ANY)
     return pl.pallas_call(
-        functools.partial(contribution_kernel, own_tiles, left_tiles, chunk),
-        out_shape=jax.ShapeDtypeStruct((fronts, width, width), jnp.float32),
+        functools.partial(contribution_kernel, own_tiles, left_tiles, first_slot, len(halo)),
+        out_shape=jax.ShapeDtypeStruct((fronts, width, mine_width), jnp.float32),
         grid_spec=pltpu.PrefetchScalarGridSpec(
             num_scalar_prefetch=1,
             grid=(fronts,),
-            in_specs=[
-                pl.BlockSpec(memory_space=pltpu.VMEM),
-                pl.BlockSpec(memory_space=pl.ANY),
-                pl.BlockSpec(memory_space=pl.ANY),
-            ],
-            out_specs=pl.BlockSpec((1, width, width), lambda f, info: (f, 0, 0)),
+            in_specs=[pl.BlockSpec(memory_space=pltpu.VMEM)] + [anywhere] * (1 + len(halo) + len(after)),
+            out_specs=pl.BlockSpec((1, width, mine_width), lambda f, info: (f, 0, 0)),
             scratch_shapes=[
-                pltpu.VMEM((fronts, width, width), jnp.float32),
-                pltpu.VMEM((width, depth), jnp.bfloat16),
-                pltpu.VMEM((width, depth), jnp.bfloat16),
+                pltpu.VMEM((fronts, mine_width, width), jnp.float32),
+                pltpu.VMEM((mine_width, depth), jnp.bfloat16),
+                pltpu.VMEM((mine_width, depth), jnp.bfloat16),
                 pltpu.VMEM((width, depth), jnp.bfloat16),
                 pltpu.VMEM((width, depth), jnp.bfloat16),
                 pltpu.SemaphoreType.DMA((fronts,)),
             ],
         ),
-        compiler_params=pltpu.CompilerParams(vmem_limit_bytes=60 * 2**20),
+        compiler_params=pltpu.CompilerParams(vmem_limit_bytes=44 * 2**20),
         cost_estimate=pl.CostEstimate(
-            flops=6 * fronts * width * width * depth, bytes_accessed=8 * fronts * width * width, transcendentals=0
+            flops=6 * fronts * width * mine_width * depth,
+            bytes_accessed=8 * fronts * width * mine_width,
+            transcendentals=0,
         ),
         name="contribute",
-    )(info, panel, own, halo)
-
-
-def assemble_kernel(fronts, slots, fetch, valid, target, *refs):
-    blocks, out = refs[:fronts], refs[fronts]
+    )(info, panel, own, *halo, *after)
+
+
+def assemble_kernel(fronts, firsts, fetch, valid, target, *refs):
+    blocks, out = refs[:-1], refs[-1]
     here = pl.program_id(0)
     out[...] = jnp.zeros_like(out)
     for k in range(fronts):
 
         @pl.when(valid[k, here] > 0)
         def _():
-            for slot in range(slots):
-                place = target[k, slot]
-
-                @pl.when(place >= 0)
-                def _():
-                    at = pl.ds(pl.multiple_of(place * TILE, TILE), TILE)
-                    out[:, at] = out[:, at] + blocks[k][0, :, slot * TILE : (slot + 1) * TILE]
-
-
-def assemble(routed, fetch, valid, target, block_width):
-    fronts, width, _ = routed.shape
-    slots = width // TILE
+            for part, first in enumerate(firsts):
+                block = blocks[part * fronts + k]
+                for slot in range(block.shape[2] // TILE):
+                    place = target[k, first + slot]
+
+                    @pl.when(place >= 0)
+                    def _():
+                        at = pl.ds(pl.multiple_of(place * TILE, TILE), TILE)
+                        out[:, at] = out[:, at] + block[0, :, slot * TILE : (slot + 1) * TILE]
+
+
+def assemble(parts, firsts, fetch, valid, target, block_width):
+    fronts, width, part_width = parts[0].shape
     order = block_width * TILE
 
     def spec(k):
-        return pl.BlockSpec((1, TILE, width), lambda a, fetch, valid, target: (k, fetch[k, a], 0))
+        return pl.BlockSpec((1, TILE, part_width), lambda a, fetch, valid, target: (k, fetch[k, a], 0))
 
     return pl.pallas_call(
-        functools.partial(assemble_kernel, fronts, slots),
+        functools.partial(assemble_kernel, fronts, firsts),
         out_shape=jax.ShapeDtypeStruct((order, order), jnp.float32),
         grid_spec=pltpu.PrefetchScalarGridSpec(
             num_scalar_prefetch=3,
             grid=(block_width,),
-            in_specs=[spec(k) for k in range(fronts)],
+            in_specs=[spec(k) for _ in parts for k in range(fronts)],
             out_specs=pl.BlockSpec((TILE, order), lambda a, fetch, valid, target: (a, 0)),
         ),
         compiler_params=pltpu.CompilerParams(vmem_limit_bytes=48 * 2**20),
@@ -220,17 +214,17 @@
             flops=0, bytes_accessed=4 * (fronts * width * width + order * order), transcendentals=0
         ),
         name="assemble",
-    )(fetch, valid, target, *([routed] * fronts))
-
-
-def exchange_halo(own, row_count, own_tiles, slots, tiles):
+    )(fetch, valid, target, *[part for part in parts for _ in range(fronts)])
+
+
+def exchange_halo(own, later, row_count, own_tiles, slots, tiles):
     left, right = [], []
     for r in range(row_count):
         left.append(own_tiles * r - max(0, tiles - slots * (row_count - r)))
         right.append(min(tiles, slots * (r + 1)) - own_tiles * (r + 1))
 
     def tile_row(index):
-        return lax.slice_in_dim(own, index * TILE, (index + 1) * TILE, axis=0)
+        return lax.slice_in_dim(own, index * TILE, (index + 1) * TILE, axis=0) + later
 
     pieces = []
     for t in range(1, max(left) + 1):
@@ -241,7 +235,16 @@
         distance = 1 + t // own_tiles
         pairs = [(r + distance, r) for r in range(row_count) if right[r] > t]
         pieces.append(lax.ppermute(tile_row(t % own_tiles), "row", pairs))
-    return jnp.concatenate(pieces, axis=0), max(left)
+    return pieces, max(left)
+
+
+def always_own(row_count, own_tiles, slots, tiles, first_slot, chunk):
+    for r in range(row_count):
+        least = max(0, tiles - slots * (row_count - r)) + first_slot - own_tiles * r
+        most = min(tiles - slots, slots * r) + first_slot + chunk - 1 - own_tiles * r
+        if least < 0 or most >= own_tiles:
+            return False
+    return True
 
 
 def local(pivot_block, panel_rows, update_block, tile_map):
@@ -260,8 +263,6 @@
 
     pivot_whole = lax.all_gather(pivot_block[0], "row", axis=0, tiled=True)
     panel_whole = lax.all_gather(panel_rows[0], "row", axis=0, tiled=True)
-    halo, left_tiles = exchange_halo(update_block[0], row_count, own_tiles, slots, tiles)
-
     def first_tile(maps, block):
         count = jnp.sum((maps // row_width < block).astype(jnp.int32), axis=-1)
         return jnp.minimum(count, tiles - slots)
@@ -289,12 +290,32 @@
     target = jnp.where((target >= 0) & (target < row_width), target, -1)
 
     lower, inverse = factor_pivot(pivot_whole)
+    later = 0.0 * inverse[0, 0]
+    halo, left_tiles = exchange_halo(update_block[0], later, row_count, own_tiles, slots, tiles)
     panel = mul(panel_whole, inverse, NT)
-    source = contribute(
-        panel, update_block[0], halo, info, front_count, slots, own_tiles, left_tiles
-    )
-    routed = lax.all_to_all(source, "front", split_axis=0, concat_axis=0, tiled=True)
-    parent = assemble(routed, fetch, valid, target, row_width)
+    chunk = slots // 3 if slots % 3 == 0 else slots
+    firsts = list(range(0, slots, chunk))
+    if len(firsts) == 3:
+        firsts = [firsts[1], firsts[0], firsts[2]]
+    parts, after = [], []
+    for first_slot in firsts:
+        inner = always_own(row_count, own_tiles, slots, tiles, first_slot, chunk)
+        source = contribute(
+            panel,
+            update_block[0],
+            [] if inner else halo,
+            after,
+            info,
+            front_count,
+            slots,
+            first_slot,
+            chunk,
+            own_tiles,
+            left_tiles,
+        )
+        after = [source]
+        parts.append(lax.all_to_all(source, "front", split_axis=0, concat_axis=0, tiled=True))
+    parent = assemble(parts, firsts, fetch, valid, target, row_width)
     lower_own = lax.dynamic_slice_in_dim(lower, row_me * pivot_share, pivot_share, 0)
     panel_own = lax.dynamic_slice_in_dim(panel, row_me * own_rows, own_rows, 0)
     return (lower_own[None], panel_own[None], parent[None])

time: 694 us -> 645 us (0.929)
  blocking collectives: 0 us -> 161 us
  waiting for transfers between devices: 452 us -> 293 us
  starting transfers between devices: 74.8 us -> 21.4 us
  local copies, waits for them, and re-layouts: 34.7 us -> 12.9 us
  Pallas kernels: 97.5 us -> 109 us
  other arithmetic: 2.26 us -> 10.4 us
    all_to_all x1 -> x2, waiting for transfers between devices: 451 us -> 244 us  [local(): lax.all_to_all(source, 'front', split_axis=0, concat_axis=0, tiled=True)]
    all_to_all x0 -> x1, blocking collectives: none -> 161 us  [local(): lax.all_to_all(source, 'front', split_axis=0, concat_axis=0, tiled=True)]
    ppermute x3, starting transfers between devices: 61.7 us -> 7.67 us  [exchange_halo(): pieces.append(lax.ppermute(tile_row(t % own_tiles), 'row', pairs))]
    all_gather x1, waiting for transfers between devices: 0.01 us -> 27.3 us  [local(): panel_whole = lax.all_gather(panel_rows[0], 'row', axis=0, tiled=True)]
    all_gather x1, waiting for transfers between devices: 0.01 us -> 16.6 us  [local(): pivot_whole = lax.all_gather(pivot_block[0], 'row', axis=0, tiled=True)]
    pallas_call x1 -> x3, Pallas kernels: 34.4 us -> 46.5 us  [contribute(): pl.pallas_call(functools.partial(contribution_kernel, own_tiles, left_til...]
    unnamed x11 -> x10, local copies, waits for them, and re-layouts: 16.8 us -> 5.48 us
    slice x1, local copies, waits for them, and re-layouts: 9.46 us -> 0.51 us  [local(): later = 0.0 * inverse[0, 0]]
  transfers between devices with their start and end apart: 9 -> 10, of which waited for: 1 -> 6; matrix products, arithmetic and copies ran while one was open for 5% -> 3% of each run, Pallas kernels for 5% -> 10%
where the time goes in v2:
time: 645 us; the launch traced here: 640 us
  waiting for transfers between devices  293 us (45%)
  blocking collectives  161 us (25%)
  Pallas kernels  109 us (17%)
  starting transfers between devices  21.4 us (3%)
  matrix products  17.2 us (3%)
  between operations  15.6 us (2%)
  local copies, waits for them, and re-layouts  12.9 us (2%)
  other arithmetic  10.4 us (2%)
    all_to_all x2, waiting for transfers between devices, local(): lax.all_to_all(source, 'front', split_axis=0, concat_axis=0, tiled=True)  244 us
    all_to_all x1, blocking collectives, local(): lax.all_to_all(source, 'front', split_axis=0, concat_axis=0, tiled=True)  161 us
    pallas_call x3, Pallas kernels, contribute(): pl.pallas_call(functools.partial(contribution_kernel, own_tiles, left_til...  46.5 us
    pallas_call x1, Pallas kernels, factor_pivot(): pl.pallas_call(pivot_kernel, out_shape=[jax.ShapeDtypeStruct((size, size)...  31.4 us
    pallas_call x1, Pallas kernels, assemble(): pl.pallas_call(functools.partial(assemble_kernel, fronts, firsts), out_sh...  30.8 us
    all_gather x1, waiting for transfers between devices, local(): panel_whole = lax.all_gather(panel_rows[0], 'row', axis=0, tiled=True)  27.3 us
    dot_general x1, matrix products, mul(): lax.dot_general(left, right, dims, precision=HIGHEST, preferred_element_t...  17.2 us
    all_gather x1, waiting for transfers between devices, local(): pivot_whole = lax.all_gather(pivot_block[0], 'row', axis=0, tiled=True)  16.6 us
  transfers between devices with their start and end apart: 10, of which 6 were waited for; matrix products, arithmetic and copies ran while one was open for 3% of the time, Pallas kernels for 10%

profile of v2, /device:TPU:5, one launch (start us, length us, event | category | flops | bytes accessed | tf_op | source)
XLA Modules:
  0.0 640.5 jit_solution(16242540601038940890)
XLA Ops:
  7.2 0.7 all-gather.5.cloned.1.call-update
  8.0 0.7 all-gather.7.cloned.1.call-update
  8.7 0.6 fusion.11
  10.0 0.1 convert_reduce_fusion.1
  10.1 0.1 pad_add_fusion.info
  10.2 16.6 %all-gather.5.cloned.1.call-done = f32[1,512,512]{2,1,0:T(8,128)} async-done(((f32[1,128,512]{2,1,0:T(8,128)}), f32[1,512,512]{2,1,0:T(8,128)}) %all-gather.5.cloned.1.call-update) | async-done | bytes 1048592 | tf_op jit(solution)/shard_map/all_gather | solution.py:264
  26.8 1.2 copy-done.1
  28.0 31.4 %factor_pivot.1 = (f32[512,512]{1,0:T(8,128)S(1)}, f32[512,512]{1,0:T(8,128)S(1)}) custom-call(f32[512,512]{1,0:T(8,128)S(1)} %bitcast.44), custom_call_target="tpu_custom_call" | custom-call | flops 60000002048 | bytes 3145728 | tf_op jit(solution)/shard_map/factor_pivot/pallas_call | solution.py:86
  59.4 27.3 %all-gather.7.cloned.1.call-done = f32[1,4096,512]{2,1,0:T(8,128)} async-done(((f32[1,1024,512]{2,1,0:T(8,128)}), f32[1,4096,512]{2,1,0:T(8,128)}) %all-gather.7.cloned.1.call-update) | async-done | bytes 8388624 | tf_op jit(solution)/shard_map/all_gather | solution.py:265
  86.7 17.2 %fusion.panel = f32[4096,512]{1,0:T(8,128)} fusion(f32[512,512]{1,0:T(8,128)S(1)} %get-tuple-element.7, f32[1,4096,512]{2,1,0:T(8,128)} %all-gather.7.cloned.1.call-done), kind=kOutput, calls=%fused_computation.3 | convolution fusion | flops 12884901888 | bytes 17825792 | tf_op jit(solution)/shard_map/dot_general | solution.py:19
  103.9 14.8 %contribute.3.refs_6_ = f32[4,1152,384]{2,1,0:T(8,128)S(1)} custom-call(s32[6]{0:T(128)S(1)} %pad_add_fusion.info, f32[4096,512]{1,0:T(8,128)} %fusion.panel, f32[1024,4096]{1,0:T(8,128)} %bitcast.45), custom_call_target="tpu_custom_call" | custom-call | flops 5435817984 | bytes 14155776 | tf_op jit(solution)/shard_map/contribute/pallas_call | solution.py:150
  118.8 2.9 copy-done
  121.7 5.4 all-to-all-start
  127.1 0.5 slice.28
  128.2 8.8 %add_bitcast_fusion = (f32[128,4096]{1,0:T(8,128)}, f32[128,4096]{1,0:T(8,128)}, f32[128,4096]{1,0:T(8,128)}, f32[128,4096]{1,0:T(8,128)}, f32[128,4096]{1,0:T(8,128)S(1)}, /*index=5*/f32[128,4096]{1,0:T(8,128)S(1)}) fusion(f32[1,1024,4096]{2,1,0:T(8,128)} %param.8, f32[]{:T(128)} %bitcast.13), kind=kLoop, calls=%fused_computation.5 | loop fusion | flops 3145728 | bytes 25165828 | tf_op jit(solution)/shard_map/add | solution.py:227
  137.0 2.3 collective-permute-start.5
  139.3 1.4 collective-permute-start.3
  140.7 0.8 collective-permute-start.2
  141.6 0.8 collective-permute-start.1
  142.4 1.3 collective-permute-start
  143.7 4.0 collective-permute-start.4
  147.7 1.5 collective-permute-done.refs_0_
  149.2 2.1 collective-permute-done.4.refs_4_
  151.3 1.3 copy-done.3
  152.6 15.8 %contribute.4.refs_6_ = f32[4,1152,384]{2,1,0:T(8,128)} custom-call(s32[6]{0:T(128)S(1)} %pad_add_fusion.info, f32[4096,512]{1,0:T(8,128)} %fusion.panel, f32[1024,4096]{1,0:T(8,128)} %bitcast.46, f32[128,4096]{1,0:T(8,128)S(1)} %collective-permute-done.refs_0_, f32[128,4096]{1,0:T(8,128)S(1)} %collective-permute-done.1.refs_1_, ...), custom_call_target="tpu_custom_call" | custom-call | flops 5435817984 | bytes 14155776 | tf_op jit(solution)/shard_map/contribute/pallas_call | solution.py:150
  168.4 15.9 %contribute.5 = f32[4,1152,384]{2,1,0:T(8,128)} custom-call(s32[6]{0:T(128)S(1)} %pad_add_fusion.info, f32[4096,512]{1,0:T(8,128)} %fusion.panel, f32[1024,4096]{1,0:T(8,128)} %bitcast.47, f32[128,4096]{1,0:T(8,128)S(1)} %collective-permute-done.refs_0_, f32[128,4096]{1,0:T(8,128)S(1)} %collective-permute-done.1.refs_1_, ...), custom_call_target="tpu_custom_call" | custom-call | flops 5435817984 | bytes 14155776 | tf_op jit(solution)/shard_map/contribute/pallas_call | solution.py:150
  184.3 97.7 %all-to-all-done.refs_0_.refs_1_.refs_2_.refs_3_ = f32[4,1152,384]{2,1,0:T(8,128)} async-done(((f32[4,1152,384]{2,1,0:T(8,128)}), f32[4,1152,384]{2,1,0:T(8,128)}, u32[]{:S(2)}, u32[]{:S(2)}) %all-to-all-start) | async-done | bytes 7077920 | tf_op jit(solution)/shard_map/all_to_all | solution.py:317
  282.0 161.0 %all_to_all.15.refs_8_.refs_9_.refs_10_.refs_11_ = f32[4,1152,384]{2,1,0:T(8,128)} all-to-all(f32[4,1152,384]{2,1,0:T(8,128)} %contribute.5), channel_id=1, replica_groups=mesh['front'=4,'row'=4,'col'=2] {'front'}, dimensions={0} | all-to-all | bytes 14155776 | tf_op jit(solution)/shard_map/all_to_all | solution.py:317
  443.0 5.4 all-to-all-start.1
  448.4 0.6 gather_fusion
  449.0 0.1 add_select_fusion
  449.1 0.1 convert_reduce_fusion.2
  449.2 0.1 bitcast_or_fusion.1
  449.3 0.1 reshape.109
  449.4 1.1 gather_fusion.1
  450.5 0.1 reshape.112
  450.5 0.1 bitcast_or_fusion
  450.6 0.1 reshape.114
  450.7 1.1 gather_fusion.2
  451.8 0.1 reshape.117
  451.9 0.1 copy.7
  452.0 0.1 fusion.2
  452.1 0.1 convert_reduce_fusion
  452.2 0.1 and_select_fusion.target
  452.3 0.7 dynamic-slice_bitcast_fusion.1
  453.0 3.1 dynamic-slice_bitcast_fusion
  456.1 146.7 %all-to-all-done.1.refs_4_.refs_5_.refs_6_.refs_7_ = f32[4,1152,384]{2,1,0:T(8,128)} async-done(((f32[4,1152,384]{2,1,0:T(8,128)}), f32[4,1152,384]{2,1,0:T(8,128)}, u32[]{:S(2)}, u32[]{:S(2)}) %all-to-all-start.1) | async-done | bytes 7077920 | tf_op jit(solution)/shard_map/all_to_all | solution.py:317
  602.9 30.8 %assemble.1 = f32[3072,3072]{1,0:T(8,128)} custom-call(s32[4,24]{1,0:T(4,128)S(1)} %add_clamp_fusion.fetch, s32[4,24]{1,0:T(4,128)S(1)} %convert_element_type.20.valid, s32[4,9]{1,0:T(4,128)S(1)} %and_select_fusion.target, f32[4,1152,384]{2,1,0:T(8,128)} %all-to-all-done.refs_0_.refs_1_.refs_2_.refs_3_, ...), custom_call_target="tpu_custom_call" | custom-call | bytes 58982400 | tf_op jit(solution)/shard_map/assemble/pallas_call | solution.py:203
  (23 shorter events, 0.2 us)
Async XLA Ops:
  7.2 1.5 copy-start.4
  7.2 19.6 %all-gather.5.cloned.1.call-start = ((), (), s32[]{:S(2)}) async-start(), calls=%async_computation.3 | async-start | bytes 1310720 | tf_op jit(solution)/shard_map/all_gather | solution.py:264
  7.9 78.8 %all-gather.7.cloned.1.call-start = ((), (), s32[]{:S(2)}) async-start(), calls=%async_computation.4 | async-start | bytes 10485760 | tf_op jit(solution)/shard_map/all_gather | solution.py:265
  26.8 1.2 copy-start.1
  118.7 2.9 copy-start
  121.7 160.3 %all-to-all-start = ((f32[4,1152,384]{2,1,0:T(8,128)}), f32[4,1152,384]{2,1,0:T(8,128)}, u32[]{:S(2)}, u32[]{:S(2)}) async-start(f32[4,1152,384]{2,1,0:T(8,128)} %copy-done), calls=%async_computation | async-start | bytes 14155776 | tf_op jit(solution)/shard_map/all_to_all | solution.py:317
  137.0 6.6 %collective-permute-start.5 = (f32[128,4096]{1,0:T(8,128)}, f32[128,4096]{1,0:T(8,128)S(1)}, u32[]{:S(2)}, u32[]{:S(2)}) collective-permute-start(f32[128,4096]{1,0:T(8,128)} %get-tuple-element.14), channel_id=1, source_target_pairs={{6,4},{7,5},{14,12},{15,13},{22,20},{23,21},{30,28},{31,29}} | collective-permute-start | bytes 6291464 | tf_op jit(solution)/shard_map/ppermute | solution.py:237
  139.3 8.3 %collective-permute-start.3 = (f32[128,4096]{1,0:T(8,128)}, f32[128,4096]{1,0:T(8,128)S(1)}, u32[]{:S(2)}, u32[]{:S(2)}) collective-permute-start(f32[128,4096]{1,0:T(8,128)} %get-tuple-element.15), channel_id=1, source_target_pairs={{2,0},{4,2},{6,4},{3,1},{5,3},{7,5},{10,8},{12,10},{14,12},{11,9},... | collective-permute-start | bytes 6291464 | tf_op jit(solution)/shard_map/ppermute | solution.py:237
  140.7 6.9 %collective-permute-start.2 = (f32[128,4096]{1,0:T(8,128)}, f32[128,4096]{1,0:T(8,128)S(1)}, u32[]{:S(2)}, u32[]{:S(2)}) collective-permute-start(f32[128,4096]{1,0:T(8,128)} %get-tuple-element.16), channel_id=1, source_target_pairs={{0,2},{1,3},{8,10},{9,11},{16,18},{17,19},{24,26},{25,27}} | collective-permute-start | bytes 6291464 | tf_op jit(solution)/shard_map/ppermute | solution.py:233
  141.6 6.1 collective-permute-start.1
  142.4 6.9 %collective-permute-start = (f32[128,4096]{1,0:T(8,128)S(1)}, f32[128,4096]{1,0:T(8,128)S(1)}, u32[]{:S(2)}, u32[]{:S(2)}) collective-permute-start(f32[128,4096]{1,0:T(8,128)S(1)} %get-tuple-element.18), channel_id=1, source_target_pairs={{0,2},{2,4},{4,6},{1,3},{3,5},{5,7},{8,10},{10,12},{12,14},{9,11},... | collective-permute-start | bytes 6291464 | tf_op jit(solution)/shard_map/ppermute | solution.py:233
  143.7 7.6 %copy-start.2 = (f32[128,4096]{1,0:T(8,128)}, f32[128,4096]{1,0:T(8,128)S(1)}, u32[]{:S(2)}) copy-start(f32[128,4096]{1,0:T(8,128)S(1)} %collective-permute-done.5.refs_5_) | copy-start | bytes 6291460
  143.7 7.6 %collective-permute-start.4 = (f32[128,4096]{1,0:T(8,128)S(1)}, f32[128,4096]{1,0:T(8,128)S(1)}, u32[]{:S(2)}, u32[]{:S(2)}) collective-permute-start(f32[128,4096]{1,0:T(8,128)S(1)} %get-tuple-element.19), channel_id=1, source_target_pairs={{4,2},{6,4},{5,3},{7,5},{12,10},{14,12},{13,11},{15,13},{20,18},{2... | collective-permute-start | bytes 6291464 | tf_op jit(solution)/shard_map/ppermute | solution.py:237
  151.3 1.3 copy-start.3
  443.0 159.9 %all-to-all-start.1 = ((f32[4,1152,384]{2,1,0:T(8,128)}), f32[4,1152,384]{2,1,0:T(8,128)}, u32[]{:S(2)}, u32[]{:S(2)}) async-start(f32[4,1152,384]{2,1,0:T(8,128)} %contribute.4.refs_6_), calls=%async_computation.1 | async-start | bytes 14155776 | tf_op jit(solution)/shard_map/all_to_all | solution.py:317
Sparse Core Ops, SparseCore 0:
  9.6 17.1 all-gather.4
  28.3 58.3 all-gather.6
